TPU v7x, 256 devices: a whole 4x4x8 slice. The times are simulated.
256 devices in a mesh: gx: 16 (over y, x), gy: 16 (over z, core).
Axes of the slice: x: 4, y: 4, z: 8, core: 2. Of those that a mesh axis runs over, the one named last changes fastest.
Arguments:
- charges: bfloat16 [16, 16, 512, 256], P('gx', 'gy'), may hold values from -6 to 6
- near_blocks: bfloat16 [16, 16, 3, 3, 512, 512], P('gx', 'gy'), may hold values from -0.09375 to 0.09375
- basis: bfloat16 [16, 16, 512, 128], P('gx', 'gy'), may hold values from -0.25 to 0.25
- transfer: bfloat16 [16, 16, 128, 128], P('gx', 'gy'), may hold values from -0.25 to 0.25
- coupling_leaf: bfloat16 [16, 16, 27, 128, 128], P('gx', 'gy'), may hold values from -0.109375 to 0.109375
- coupling_top: bfloat16 [16, 16, 27, 32, 128], P('gx', 'gy'), may hold values from -0.109375 to 0.109375
Outputs:
- potentials: bfloat16 [16, 16, 512, 256], P('gx', 'gy')
All inputs are finite; a program needn't handle non-finite values.
Results may differ from a plain program's by a relative error of at most 0.0085.
Values may be sent and summed in bfloat16 or wider, within the bound.
A program may use at most 128 MiB of HBM per device.

v0:
```python
import jax
import jax.numpy as jnp
import numpy as np
from jax import lax
from jax.sharding import PartitionSpec as P


def passed_along(block, axis, distance):
    devices = range(lax.axis_size(axis))
    route = [(i - distance, i) for i in devices if i - distance in devices]
    return lax.ppermute(block, axis, route)


def swapped(shard, axis, apart):
    return lax.ppermute(shard, axis, [(i, i ^ 1 << apart) for i in range(lax.axis_size(axis))])


def extended(shard, sides, width):
    for axis, dim in sides:
        devices, length = (lax.axis_size(axis), shard.shape[dim])
        up = [(i, (i + 1) % devices) for i in range(devices - 1)]
        down = [(j, i) for i, j in up]
        last = lax.slice_in_dim(shard, length - width, length, axis=dim)
        initial = lax.slice_in_dim(shard, 0, width, axis=dim)
        before = lax.ppermute(last, axis, up)
        after = lax.ppermute(initial, axis, down)
        shard = jnp.concatenate([before, shard, after], axis=dim)
    return shard


def cousin_table():
    table = np.zeros((2, 2, 27), np.int32)
    for parity_a in range(2):
        for parity_b in range(2):
            slot = 0
            for big_a in range(6):
                for big_b in range(6):
                    off_a = big_a - 2 - parity_a
                    off_b = big_b - 2 - parity_b
                    if abs(off_a) <= 1 and abs(off_b) <= 1:
                        continue
                    table[parity_a, parity_b, slot] = (off_a + 3) * 7 + (off_b + 3)
                    slot += 1
    return table


def window(moments, stride):
    columns = []
    for offset in range(-3, 4):
        if offset == 0:
            columns.append(moments)
        else:
            columns.append(passed_along(moments, "gx", -stride * offset))
    stacked = jnp.stack(columns)
    pieces = []
    for offset in range(-3, 4):
        if offset == 0:
            pieces.append(stacked)
        else:
            pieces.append(passed_along(stacked, "gy", -stride * offset))
    return jnp.stack(pieces, axis=1)


def cousins(moments, stride, parity_a, parity_b):
    grid = window(moments, stride)
    flat = grid.reshape((49,) + moments.shape)
    slots = jnp.asarray(cousin_table())[parity_a, parity_b]
    return jnp.take(flat, slots, axis=0)


def shards(charges, near_blocks, basis, transfer, coupling_leaf, coupling_top):
    f32 = jnp.float32
    local_x = charges[0, 0]
    leaf_basis = basis[0, 0]
    leaf_transfer = transfer[0, 0]
    moments = jnp.einsum("jk,jn->kn", leaf_basis, local_x, preferred_element_type=f32).astype(
        jnp.bfloat16
    )
    term = jnp.einsum("rk,rn->kn", leaf_transfer, moments, preferred_element_type=f32)
    paired = term + swapped(term.astype(jnp.bfloat16), "gx", 0).astype(term.dtype)
    top = (paired + swapped(paired.astype(jnp.bfloat16), "gy", 0).astype(paired.dtype)).astype(
        jnp.bfloat16
    )
    index_x = lax.axis_index("gx")
    index_y = lax.axis_index("gy")
    even_x = index_x % 2 == 0
    even_y = index_y % 2 == 0
    leaf_sources = cousins(moments, 1, index_x % 2, index_y % 2)
    local_leaf = jnp.einsum(
        "skr,srn->kn", coupling_leaf[0, 0], leaf_sources, preferred_element_type=f32
    )
    top_sources = cousins(top, 2, index_x // 2 % 2, index_y // 2 % 2)
    quarter = jnp.einsum(
        "skr,srn->kn", coupling_top[0, 0], top_sources, preferred_element_type=f32
    ).astype(jnp.bfloat16)
    partner = swapped(quarter, "gy", 0)
    half = jnp.where(
        even_y, jnp.concatenate([quarter, partner], 0), jnp.concatenate([partner, quarter], 0)
    )
    other_half = swapped(half, "gx", 0)
    full_top = jnp.where(
        even_x, jnp.concatenate([half, other_half], 0), jnp.concatenate([other_half, half], 0)
    )
    total = (local_leaf + jnp.dot(leaf_transfer, full_top, preferred_element_type=f32)).astype(
        jnp.bfloat16
    )
    neighbours = extended(charges, (("gx", 0), ("gy", 1)), 1)
    near_sum = jnp.einsum(
        "uvij,uvjn->in", near_blocks[0, 0], neighbours, preferred_element_type=f32
    )
    result = near_sum + jnp.dot(leaf_basis, total, preferred_element_type=f32)
    return result.astype(jnp.bfloat16)[None, None]


def solution(mesh):
    return jax.shard_map(
        shards,
        mesh=mesh,
        in_specs=(
            P("gx", "gy", None, None),
            P("gx", "gy", None, None, None, None),
            P("gx", "gy", None, None),
            P("gx", "gy", None, None),
            P("gx", "gy", None, None, None),
            P("gx", "gy", None, None, None),
        ),
        out_specs=P("gx", "gy", None, None),
        check_vma=False,
    )
```

profile of v0, /device:TPU:80, one launch (start us, length us, event | category | flops | bytes accessed | tf_op | source)
XLA Modules:
  0.0 221.0 jit_solution(14948425568137584370)
XLA Ops:
  1.3 4.7 %collective-permute-start.4 = (bf16[128,256]{1,0:T(8,128)(2,1)S(1)}, bf16[128,256]{1,0:T(8,128)(2,1)S(1)}, u32[]{:S(2)}, u32[]{:S(2)}) collective-permute-start(bf16[128,256]{1,0:T(8,128)(2,1)S(1)} %convolution_convert_fusion), channel_id=1, source_target_pairs={{0,48},{16,64},{32,80},{48,96},{64,112},{80,128},{96,144},{112,160... | collective-permute-start | bytes 196616 | tf_op jit(solution)/shard_map/ppermute | solution.py:11
  6.0 3.4 %collective-permute-start.5 = (bf16[128,256]{1,0:T(8,128)(2,1)S(1)}, bf16[128,256]{1,0:T(8,128)(2,1)S(1)}, u32[]{:S(2)}, u32[]{:S(2)}) collective-permute-start(bf16[128,256]{1,0:T(8,128)(2,1)S(1)} %convolution_convert_fusion), channel_id=1, source_target_pairs={{0,32},{16,48},{32,64},{48,80},{64,96},{80,112},{96,128},{112,144}... | collective-permute-start | bytes 196616 | tf_op jit(solution)/shard_map/ppermute | solution.py:11
  12.2 5.2 %collective-permute-start.7 = (bf16[128,256]{1,0:T(8,128)(2,1)S(1)}, bf16[128,256]{1,0:T(8,128)(2,1)S(1)}, u32[]{:S(2)}, u32[]{:S(2)}) collective-permute-start(bf16[128,256]{1,0:T(8,128)(2,1)S(1)} %convolution_convert_fusion), channel_id=1, source_target_pairs={{16,0},{32,16},{48,32},{64,48},{80,64},{96,80},{112,96},{128,112},... | collective-permute-start | bytes 196616 | tf_op jit(solution)/shard_map/ppermute | solution.py:11
  27.6 4.5 %collective-permute-start = (bf16[1,1,512,256]{2,3,1,0:T(8,128)(2,1)S(1)}, bf16[1,1,512,256]{2,3,1,0:T(8,128)(2,1)S(1)}, u32[]{:S(2)}, u32[]{:S(2)}) collective-permute-start(bf16[1,1,512,256]{2,3,1,0:T(8,128)(2,1)S(1)} %copy.13), channel_id=1, source_target_pairs={{0,16},{16,32},{32,48},{48,64},{64,80},{80,96},{96,112},{112,128},... | collective-permute-start | bytes 786440 | tf_op jit(solution)/shard_map/ppermute | solution.py:25
  37.0 3.8 %collective-permute-start.18 = (bf16[128,256]{0,1:T(8,128)(2,1)S(1)}, bf16[128,256]{0,1:T(8,128)(2,1)S(1)}, u32[]{:S(2)}, u32[]{:S(2)}) collective-permute-start(bf16[128,256]{0,1:T(8,128)(2,1)S(1)} %add_convert_fusion), channel_id=1, source_target_pairs={{0,96},{16,112},{32,128},{48,144},{64,160},{80,176},{96,192},{112,... | collective-permute-start | bytes 196616 | tf_op jit(solution)/shard_map/ppermute | solution.py:11
  44.2 5.0 %collective-permute-start.11 = (bf16[7,128,256]{2,1,0:T(8,128)(2,1)S(1)}, bf16[7,128,256]{2,1,0:T(8,128)(2,1)S(1)}, u32[]{:S(2)}, u32[]{:S(2)}) collective-permute-start(bf16[7,128,256]{2,1,0:T(8,128)(2,1)S(1)} %bitcast_dynamic-update-slice_fusion.21), channel_id=1, source_target_pairs={{0,2},{1,3},{2,4},{3,5},{4,6},{5,7},{6,8},{7,9},{8,10},{9,11},{10,... | collective-permute-start | bytes 1376264 | tf_op jit(solution)/shard_map/ppermute | solution.py:11
  51.2 4.8 %collective-permute-done.19 = bf16[128,256]{0,1:T(8,128)(2,1)S(1)} collective-permute-done((bf16[128,256]{0,1:T(8,128)(2,1)S(1)}, bf16[128,256]{0,1:T(8,128)(2,1)S(1)}, u32[]{:S(2)}, u32[]{:S(2)}) %collective-permute-start.19) | collective-permute-done | bytes 65568 | tf_op jit(solution)/shard_map/ppermute | solution.py:11
  55.9 3.8 %collective-permute-start.20 = (bf16[128,256]{0,1:T(8,128)(2,1)S(1)}, bf16[128,256]{0,1:T(8,128)(2,1)S(1)}, u32[]{:S(2)}, u32[]{:S(2)}) collective-permute-start(bf16[128,256]{0,1:T(8,128)(2,1)S(1)} %add_convert_fusion), channel_id=1, source_target_pairs={{0,32},{16,48},{32,64},{48,80},{64,96},{80,112},{96,128},{112,144}... | collective-permute-start | bytes 196616 | tf_op jit(solution)/shard_map/ppermute | solution.py:11
  59.7 4.8 %collective-permute-done.20 = bf16[128,256]{0,1:T(8,128)(2,1)S(1)} collective-permute-done((bf16[128,256]{0,1:T(8,128)(2,1)S(1)}, bf16[128,256]{0,1:T(8,128)(2,1)S(1)}, u32[]{:S(2)}, u32[]{:S(2)}) %collective-permute-start.20) | collective-permute-done | bytes 65568 | tf_op jit(solution)/shard_map/ppermute | solution.py:11
  64.5 4.3 %collective-permute-start.21 = (bf16[128,256]{0,1:T(8,128)(2,1)S(1)}, bf16[128,256]{0,1:T(8,128)(2,1)S(1)}, u32[]{:S(2)}, u32[]{:S(2)}) collective-permute-start(bf16[128,256]{0,1:T(8,128)(2,1)S(1)} %add_convert_fusion), channel_id=1, source_target_pairs={{32,0},{48,16},{64,32},{80,48},{96,64},{112,80},{128,96},{144,112}... | collective-permute-start | bytes 196616 | tf_op jit(solution)/shard_map/ppermute | solution.py:11
  74.8 3.5 %collective-permute-done.22 = bf16[128,256]{0,1:T(8,128)(2,1)S(1)} collective-permute-done((bf16[128,256]{0,1:T(8,128)(2,1)S(1)}, bf16[128,256]{0,1:T(8,128)(2,1)S(1)}, u32[]{:S(2)}, u32[]{:S(2)}) %collective-permute-start.22) | collective-permute-done | bytes 65568 | tf_op jit(solution)/shard_map/ppermute | solution.py:11
  78.3 4.6 %collective-permute-start.23 = (bf16[128,256]{0,1:T(8,128)(2,1)S(1)}, bf16[128,256]{0,1:T(8,128)(2,1)S(1)}, u32[]{:S(2)}, u32[]{:S(2)}) collective-permute-start(bf16[128,256]{0,1:T(8,128)(2,1)S(1)} %add_convert_fusion), channel_id=1, source_target_pairs={{96,0},{112,16},{128,32},{144,48},{160,64},{176,80},{192,96},{208,... | collective-permute-start | bytes 196616 | tf_op jit(solution)/shard_map/ppermute | solution.py:11
  82.9 3.9 %collective-permute-done.23 = bf16[128,256]{0,1:T(8,128)(2,1)S(1)} collective-permute-done((bf16[128,256]{0,1:T(8,128)(2,1)S(1)}, bf16[128,256]{0,1:T(8,128)(2,1)S(1)}, u32[]{:S(2)}, u32[]{:S(2)}) %collective-permute-start.23) | collective-permute-done | bytes 65568 | tf_op jit(solution)/shard_map/ppermute | solution.py:11
  88.8 3.6 %collective-permute-start.13 = (bf16[7,128,256]{2,1,0:T(8,128)(2,1)S(1)}, bf16[7,128,256]{2,1,0:T(8,128)(2,1)S(1)}, u32[]{:S(2)}, u32[]{:S(2)}) collective-permute-start(bf16[7,128,256]{2,1,0:T(8,128)(2,1)S(1)} %bitcast_dynamic-update-slice_fusion.21), channel_id=1, source_target_pairs={{1,0},{2,1},{3,2},{4,3},{5,4},{6,5},{7,6},{8,7},{9,8},{10,9},{11,1... | collective-permute-start | bytes 1376264 | tf_op jit(solution)/shard_map/ppermute | solution.py:11
  98.1 6.4 %collective-permute-start.24 = (bf16[7,128,256]{1,2,0:T(8,128)(2,1)S(1)}, bf16[7,128,256]{1,2,0:T(8,128)(2,1)S(1)}, u32[]{:S(2)}, u32[]{:S(2)}) collective-permute-start(bf16[7,128,256]{1,2,0:T(8,128)(2,1)S(1)} %bitcast_dynamic-update-slice_fusion.14), channel_id=1, source_target_pairs={{0,6},{1,7},{2,8},{3,9},{4,10},{5,11},{6,12},{7,13},{8,14},{9,15},... | collective-permute-start | bytes 1376264 | tf_op jit(solution)/shard_map/ppermute | solution.py:11
  113.2 3.5 %collective-permute-start.27 = (bf16[7,128,256]{1,2,0:T(8,128)(2,1)S(1)}, bf16[7,128,256]{1,2,0:T(8,128)(2,1)S(1)}, u32[]{:S(2)}, u32[]{:S(2)}) collective-permute-start(bf16[7,128,256]{1,2,0:T(8,128)(2,1)S(1)} %bitcast_dynamic-update-slice_fusion.14), channel_id=1, source_target_pairs={{2,0},{3,1},{4,2},{5,3},{6,4},{7,5},{8,6},{9,7},{10,8},{11,9},{12,... | collective-permute-start | bytes 1376264 | tf_op jit(solution)/shard_map/ppermute | solution.py:11
  117.5 6.9 %collective-permute-done.24 = bf16[7,128,256]{1,2,0:T(8,128)(2,1)S(1)} collective-permute-done((bf16[7,128,256]{1,2,0:T(8,128)(2,1)S(1)}, bf16[7,128,256]{1,2,0:T(8,128)(2,1)S(1)}, u32[]{:S(2)}, u32[]{:S(2)}) %collective-permute-start.24) | collective-permute-done | bytes 458784 | tf_op jit(solution)/shard_map/ppermute | solution.py:11
  127.2 26.1 %collective-permute-done.25 = bf16[7,128,256]{1,2,0:T(8,128)(2,1)S(1)} collective-permute-done((bf16[7,128,256]{1,2,0:T(8,128)(2,1)S(1)}, bf16[7,128,256]{1,2,0:T(8,128)(2,1)S(1)}, u32[]{:S(2)}, u32[]{:S(2)}) %collective-permute-start.25) | collective-permute-done | bytes 458784 | tf_op jit(solution)/shard_map/ppermute | solution.py:11
  155.4 7.7 %collective-permute-done.26 = bf16[7,128,256]{1,2,0:T(8,128)(2,1)S(1)} collective-permute-done((bf16[7,128,256]{1,2,0:T(8,128)(2,1)S(1)}, bf16[7,128,256]{1,2,0:T(8,128)(2,1)S(1)}, u32[]{:S(2)}, u32[]{:S(2)}) %collective-permute-start.26) | collective-permute-done | bytes 458784 | tf_op jit(solution)/shard_map/ppermute | solution.py:11
  166.7 3.6 %collective-permute-start.3 = (bf16[3,1,512,256]{2,3,1,0:T(8,128)(2,1)}, bf16[3,1,512,256]{2,3,1,0:T(8,128)(2,1)}, u32[]{:S(2)}, u32[]{:S(2)}) collective-permute-start(bf16[3,1,512,256]{2,3,1,0:T(8,128)(2,1)} %pad_maximum_fusion), channel_id=1, source_target_pairs={{1,0},{2,1},{3,2},{4,3},{5,4},{6,5},{7,6},{8,7},{9,8},{10,9},{11,1... | collective-permute-start | bytes 2359304 | tf_op jit(solution)/shard_map/ppermute | solution.py:26
  171.9 19.7 %collective-permute-done.29 = bf16[7,128,256]{1,2,0:T(8,128)(2,1)S(1)} collective-permute-done((bf16[7,128,256]{1,2,0:T(8,128)(2,1)S(1)}, bf16[7,128,256]{1,2,0:T(8,128)(2,1)S(1)}, u32[]{:S(2)}, u32[]{:S(2)}) %collective-permute-start.29) | collective-permute-done | bytes 458784 | tf_op jit(solution)/shard_map/ppermute | solution.py:11
  192.5 6.1 %copy.17 = bf16[7,7,128,256]{3,2,1,0:T(8,128)(2,1)} copy(bf16[7,7,128,256]{2,3,0,1:T(8,128)(2,1)} %bitcast_dynamic-update-slice_fusion) | data formatting | bytes 6422528 | tf_op jit(solution)/shard_map/stack | solution.py:61
  204.7 4.0 %copy.16 = bf16[7,7,128,256]{3,2,1,0:T(8,128)(2,1)} copy(bf16[7,7,128,256]{3,2,0,1:T(8,128)(2,1)} %bitcast_dynamic-update-slice_fusion.7) | data formatting | bytes 6422528 | tf_op jit(solution)/shard_map/stack | solution.py:61
  215.8 4.3 %fusion.32 = bf16[1,1,512,256]{2,3,1,0:T(8,128)(2,1)S(1)} fusion(f32[256,512]{1,0:T(8,128)S(1)} %fusion.41, bf16[1,1,3,3,512,512]{5,4,3,2,1,0:T(8,128)(2,1)} %param.11, bf16[3,1,512,256]{2,3,1,0:T(8,128)(2,1)} %collective-permute-done.3, bf16[1,1,512,256]{2,3,1,0:T(8,128)(2,1)} %copy-done.4, bf16[1,1,512,256]{2,3,1,0:T(8,128)(2,1)S(1)} %copy.13, ...), kind=kOutput, calls=%fused_computation.22 | convolution fusion | flops 1212940288 | bytes 7864320 | tf_op jit(solution)/shard_map/uvij,uvjn->in/dot_general | solution.py:108
  (99 shorter events, 72.2 us)
Async XLA Ops:
  1.3 24.1 %collective-permute-start.4 = (bf16[128,256]{1,0:T(8,128)(2,1)S(1)}, bf16[128,256]{1,0:T(8,128)(2,1)S(1)}, u32[]{:S(2)}, u32[]{:S(2)}) collective-permute-start(bf16[128,256]{1,0:T(8,128)(2,1)S(1)} %convolution_convert_fusion), channel_id=1, source_target_pairs={{0,48},{16,64},{32,80},{48,96},{64,112},{80,128},{96,144},{112,160... | collective-permute-start | bytes 196616 | tf_op jit(solution)/shard_map/ppermute | solution.py:11
  6.0 21.6 %collective-permute-start.5 = (bf16[128,256]{1,0:T(8,128)(2,1)S(1)}, bf16[128,256]{1,0:T(8,128)(2,1)S(1)}, u32[]{:S(2)}, u32[]{:S(2)}) collective-permute-start(bf16[128,256]{1,0:T(8,128)(2,1)S(1)} %convolution_convert_fusion), channel_id=1, source_target_pairs={{0,32},{16,48},{32,64},{48,80},{64,96},{80,112},{96,128},{112,144}... | collective-permute-start | bytes 196616 | tf_op jit(solution)/shard_map/ppermute | solution.py:11
  9.4 22.8 %collective-permute-start.6 = (bf16[128,256]{1,0:T(8,128)(2,1)S(1)}, bf16[128,256]{1,0:T(8,128)(2,1)S(1)}, u32[]{:S(2)}, u32[]{:S(2)}) collective-permute-start(bf16[128,256]{1,0:T(8,128)(2,1)S(1)} %convolution_convert_fusion), channel_id=1, source_target_pairs={{0,16},{16,32},{32,48},{48,64},{64,80},{80,96},{96,112},{112,128},... | collective-permute-start | bytes 196616 | tf_op jit(solution)/shard_map/ppermute | solution.py:11
  12.2 23.4 %collective-permute-start.7 = (bf16[128,256]{1,0:T(8,128)(2,1)S(1)}, bf16[128,256]{1,0:T(8,128)(2,1)S(1)}, u32[]{:S(2)}, u32[]{:S(2)}) collective-permute-start(bf16[128,256]{1,0:T(8,128)(2,1)S(1)} %convolution_convert_fusion), channel_id=1, source_target_pairs={{16,0},{32,16},{48,32},{64,48},{80,64},{96,80},{112,96},{128,112},... | collective-permute-start | bytes 196616 | tf_op jit(solution)/shard_map/ppermute | solution.py:11
  22.7 13.1 %collective-permute-start.8 = (bf16[128,256]{1,0:T(8,128)(2,1)S(1)}, bf16[128,256]{1,0:T(8,128)(2,1)S(1)}, u32[]{:S(2)}, u32[]{:S(2)}) collective-permute-start(bf16[128,256]{1,0:T(8,128)(2,1)S(1)} %convolution_convert_fusion), channel_id=1, source_target_pairs={{32,0},{48,16},{64,32},{80,48},{96,64},{112,80},{128,96},{144,112}... | collective-permute-start | bytes 196616 | tf_op jit(solution)/shard_map/ppermute | solution.py:11
  25.4 15.4 %collective-permute-start.9 = (bf16[128,256]{1,0:T(8,128)(2,1)S(1)}, bf16[128,256]{1,0:T(8,128)(2,1)S(1)}, u32[]{:S(2)}, u32[]{:S(2)}) collective-permute-start(bf16[128,256]{1,0:T(8,128)(2,1)S(1)} %convolution_convert_fusion), channel_id=1, source_target_pairs={{48,0},{64,16},{80,32},{96,48},{112,64},{128,80},{144,96},{160,112... | collective-permute-start | bytes 196616 | tf_op jit(solution)/shard_map/ppermute | solution.py:11
  27.6 61.1 %collective-permute-start = (bf16[1,1,512,256]{2,3,1,0:T(8,128)(2,1)S(1)}, bf16[1,1,512,256]{2,3,1,0:T(8,128)(2,1)S(1)}, u32[]{:S(2)}, u32[]{:S(2)}) collective-permute-start(bf16[1,1,512,256]{2,3,1,0:T(8,128)(2,1)S(1)} %copy.13), channel_id=1, source_target_pairs={{0,16},{16,32},{32,48},{48,64},{64,80},{80,96},{96,112},{112,128},... | collective-permute-start | bytes 786440 | tf_op jit(solution)/shard_map/ppermute | solution.py:25
  32.2 60.2 %collective-permute-start.1 = (bf16[1,1,512,256]{2,3,1,0:T(8,128)(2,1)S(1)}, bf16[1,1,512,256]{2,3,1,0:T(8,128)(2,1)S(1)}, u32[]{:S(2)}, u32[]{:S(2)}) collective-permute-start(bf16[1,1,512,256]{2,3,1,0:T(8,128)(2,1)S(1)} %copy.13), channel_id=1, source_target_pairs={{16,0},{32,16},{48,32},{64,48},{80,64},{96,80},{112,96},{128,112},... | collective-permute-start | bytes 786440 | tf_op jit(solution)/shard_map/ppermute | solution.py:26
  37.0 12.2 %collective-permute-start.18 = (bf16[128,256]{0,1:T(8,128)(2,1)S(1)}, bf16[128,256]{0,1:T(8,128)(2,1)S(1)}, u32[]{:S(2)}, u32[]{:S(2)}) collective-permute-start(bf16[128,256]{0,1:T(8,128)(2,1)S(1)} %add_convert_fusion), channel_id=1, source_target_pairs={{0,96},{16,112},{32,128},{48,144},{64,160},{80,176},{96,192},{112,... | collective-permute-start | bytes 196616 | tf_op jit(solution)/shard_map/ppermute | solution.py:11
  40.9 54.5 %collective-permute-start.10 = (bf16[7,128,256]{2,1,0:T(8,128)(2,1)S(1)}, bf16[7,128,256]{2,1,0:T(8,128)(2,1)S(1)}, u32[]{:S(2)}, u32[]{:S(2)}) collective-permute-start(bf16[7,128,256]{2,1,0:T(8,128)(2,1)S(1)} %bitcast_dynamic-update-slice_fusion.21), channel_id=1, source_target_pairs={{0,3},{1,4},{2,5},{3,6},{4,7},{5,8},{6,9},{7,10},{8,11},{9,12},{10... | collective-permute-start | bytes 1376264 | tf_op jit(solution)/shard_map/ppermute | solution.py:11
  44.2 53.9 %collective-permute-start.11 = (bf16[7,128,256]{2,1,0:T(8,128)(2,1)S(1)}, bf16[7,128,256]{2,1,0:T(8,128)(2,1)S(1)}, u32[]{:S(2)}, u32[]{:S(2)}) collective-permute-start(bf16[7,128,256]{2,1,0:T(8,128)(2,1)S(1)} %bitcast_dynamic-update-slice_fusion.21), channel_id=1, source_target_pairs={{0,2},{1,3},{2,4},{3,5},{4,6},{5,7},{6,8},{7,9},{8,10},{9,11},{10,... | collective-permute-start | bytes 1376264 | tf_op jit(solution)/shard_map/ppermute | solution.py:11
  86.8 18.5 %collective-permute-start.12 = (bf16[7,128,256]{2,1,0:T(8,128)(2,1)S(1)}, bf16[7,128,256]{2,1,0:T(8,128)(2,1)S(1)}, u32[]{:S(2)}, u32[]{:S(2)}) collective-permute-start(bf16[7,128,256]{2,1,0:T(8,128)(2,1)S(1)} %bitcast_dynamic-update-slice_fusion.21), channel_id=1, source_target_pairs={{0,1},{1,2},{2,3},{3,4},{4,5},{5,6},{6,7},{7,8},{8,9},{9,10},{10,1... | collective-permute-start | bytes 1376264 | tf_op jit(solution)/shard_map/ppermute | solution.py:11
  88.8 21.3 %collective-permute-start.13 = (bf16[7,128,256]{2,1,0:T(8,128)(2,1)S(1)}, bf16[7,128,256]{2,1,0:T(8,128)(2,1)S(1)}, u32[]{:S(2)}, u32[]{:S(2)}) collective-permute-start(bf16[7,128,256]{2,1,0:T(8,128)(2,1)S(1)} %bitcast_dynamic-update-slice_fusion.21), channel_id=1, source_target_pairs={{1,0},{2,1},{3,2},{4,3},{5,4},{6,5},{7,6},{8,7},{9,8},{10,9},{11,1... | collective-permute-start | bytes 1376264 | tf_op jit(solution)/shard_map/ppermute | solution.py:11
  92.5 20.7 %collective-permute-start.14 = (bf16[7,128,256]{2,1,0:T(8,128)(2,1)S(1)}, bf16[7,128,256]{2,1,0:T(8,128)(2,1)S(1)}, u32[]{:S(2)}, u32[]{:S(2)}) collective-permute-start(bf16[7,128,256]{2,1,0:T(8,128)(2,1)S(1)} %bitcast_dynamic-update-slice_fusion.21), channel_id=1, source_target_pairs={{2,0},{3,1},{4,2},{5,3},{6,4},{7,5},{8,6},{9,7},{10,8},{11,9},{12,... | collective-permute-start | bytes 1376264 | tf_op jit(solution)/shard_map/ppermute | solution.py:11
  95.4 107.5 %collective-permute-start.15 = (bf16[7,128,256]{2,1,0:T(8,128)(2,1)S(1)}, bf16[7,128,256]{2,1,0:T(8,128)(2,1)}, u32[]{:S(2)}, u32[]{:S(2)}) collective-permute-start(bf16[7,128,256]{2,1,0:T(8,128)(2,1)S(1)} %bitcast_dynamic-update-slice_fusion.21), channel_id=1, source_target_pairs={{3,0},{4,1},{5,2},{6,3},{7,4},{8,5},{9,6},{10,7},{11,8},{12,9},{13... | collective-permute-start | bytes 1376264 | tf_op jit(solution)/shard_map/ppermute | solution.py:11
  98.1 26.4 %collective-permute-start.24 = (bf16[7,128,256]{1,2,0:T(8,128)(2,1)S(1)}, bf16[7,128,256]{1,2,0:T(8,128)(2,1)S(1)}, u32[]{:S(2)}, u32[]{:S(2)}) collective-permute-start(bf16[7,128,256]{1,2,0:T(8,128)(2,1)S(1)} %bitcast_dynamic-update-slice_fusion.14), channel_id=1, source_target_pairs={{0,6},{1,7},{2,8},{3,9},{4,10},{5,11},{6,12},{7,13},{8,14},{9,15},... | collective-permute-start | bytes 1376264 | tf_op jit(solution)/shard_map/ppermute | solution.py:11
  105.3 48.0 %collective-permute-start.25 = (bf16[7,128,256]{1,2,0:T(8,128)(2,1)S(1)}, bf16[7,128,256]{1,2,0:T(8,128)(2,1)S(1)}, u32[]{:S(2)}, u32[]{:S(2)}) collective-permute-start(bf16[7,128,256]{1,2,0:T(8,128)(2,1)S(1)} %bitcast_dynamic-update-slice_fusion.14), channel_id=1, source_target_pairs={{0,4},{1,5},{2,6},{3,7},{4,8},{5,9},{6,10},{7,11},{8,12},{9,13},{1... | collective-permute-start | bytes 1376264 | tf_op jit(solution)/shard_map/ppermute | solution.py:11
  110.1 53.1 %collective-permute-start.26 = (bf16[7,128,256]{1,2,0:T(8,128)(2,1)S(1)}, bf16[7,128,256]{1,2,0:T(8,128)(2,1)S(1)}, u32[]{:S(2)}, u32[]{:S(2)}) collective-permute-start(bf16[7,128,256]{1,2,0:T(8,128)(2,1)S(1)} %bitcast_dynamic-update-slice_fusion.14), channel_id=1, source_target_pairs={{0,2},{1,3},{2,4},{3,5},{4,6},{5,7},{6,8},{7,9},{8,10},{9,11},{10,... | collective-permute-start | bytes 1376264 | tf_op jit(solution)/shard_map/ppermute | solution.py:11
  113.2 53.5 %collective-permute-start.27 = (bf16[7,128,256]{1,2,0:T(8,128)(2,1)S(1)}, bf16[7,128,256]{1,2,0:T(8,128)(2,1)S(1)}, u32[]{:S(2)}, u32[]{:S(2)}) collective-permute-start(bf16[7,128,256]{1,2,0:T(8,128)(2,1)S(1)} %bitcast_dynamic-update-slice_fusion.14), channel_id=1, source_target_pairs={{2,0},{3,1},{4,2},{5,3},{6,4},{7,5},{8,6},{9,7},{10,8},{11,9},{12,... | collective-permute-start | bytes 1376264 | tf_op jit(solution)/shard_map/ppermute | solution.py:11
  124.5 46.6 %collective-permute-start.28 = (bf16[7,128,256]{1,2,0:T(8,128)(2,1)S(1)}, bf16[7,128,256]{1,2,0:T(8,128)(2,1)S(1)}, u32[]{:S(2)}, u32[]{:S(2)}) collective-permute-start(bf16[7,128,256]{1,2,0:T(8,128)(2,1)S(1)} %bitcast_dynamic-update-slice_fusion.14), channel_id=1, source_target_pairs={{4,0},{5,1},{6,2},{7,3},{8,4},{9,5},{10,6},{11,7},{12,8},{13,9},{1... | collective-permute-start | bytes 1376264 | tf_op jit(solution)/shard_map/ppermute | solution.py:11
  153.3 38.4 %collective-permute-start.29 = (bf16[7,128,256]{1,2,0:T(8,128)(2,1)S(1)}, bf16[7,128,256]{1,2,0:T(8,128)(2,1)S(1)}, u32[]{:S(2)}, u32[]{:S(2)}) collective-permute-start(bf16[7,128,256]{1,2,0:T(8,128)(2,1)S(1)} %bitcast_dynamic-update-slice_fusion.14), channel_id=1, source_target_pairs={{6,0},{7,1},{8,2},{9,3},{10,4},{11,5},{12,6},{13,7},{14,8},{15,9},... | collective-permute-start | bytes 1376264 | tf_op jit(solution)/shard_map/ppermute | solution.py:11
  163.1 52.6 %collective-permute-start.2 = (bf16[3,1,512,256]{2,3,1,0:T(8,128)(2,1)}, bf16[3,1,512,256]{2,3,1,0:T(8,128)(2,1)}, u32[]{:S(2)}, u32[]{:S(2)}) collective-permute-start(bf16[3,1,512,256]{2,3,1,0:T(8,128)(2,1)} %pad_maximum_fusion), channel_id=1, source_target_pairs={{0,1},{1,2},{2,3},{3,4},{4,5},{5,6},{6,7},{7,8},{8,9},{9,10},{10,1... | collective-permute-start | bytes 2359304 | tf_op jit(solution)/shard_map/ppermute | solution.py:25
  166.7 49.0 %collective-permute-start.3 = (bf16[3,1,512,256]{2,3,1,0:T(8,128)(2,1)}, bf16[3,1,512,256]{2,3,1,0:T(8,128)(2,1)}, u32[]{:S(2)}, u32[]{:S(2)}) collective-permute-start(bf16[3,1,512,256]{2,3,1,0:T(8,128)(2,1)} %pad_maximum_fusion), channel_id=1, source_target_pairs={{1,0},{2,1},{3,2},{4,3},{5,4},{6,5},{7,6},{8,7},{9,8},{10,9},{11,1... | collective-permute-start | bytes 2359304 | tf_op jit(solution)/shard_map/ppermute | solution.py:26
  202.5 8.8 %collective-permute-start.30 = (bf16[32,256]{1,0:T(8,128)(2,1)S(1)}, bf16[32,256]{1,0:T(8,128)(2,1)S(1)}, u32[]{:S(2)}, u32[]{:S(2)}) collective-permute-start(bf16[32,256]{1,0:T(8,128)(2,1)S(1)} %fusion.48), channel_id=1, source_target_pairs={{0,1},{1,0},{2,3},{3,2},{4,5},{5,4},{6,7},{7,6},{8,9},{9,8},{10,11... | collective-permute-start | bytes 49160 | tf_op jit(solution)/shard_map/ppermute | solution.py:15
  (14 other events, 411.9 us)
where the time goes:
time: 222 us; the launch traced here: 221 us
  starting transfers between devices  92.3 us (42%)
  waiting for transfers between devices  87 us (39%)
  local copies, waits for them, and re-layouts  29.7 us (13%)
  matrix products  9.44 us (4%)
    ppermute x24, waiting for transfers between devices, passed_along(): return lax.ppermute(block, axis, route)  81.2 us
    ppermute x24, starting transfers between devices, passed_along(): return lax.ppermute(block, axis, route)  77.7 us
    another operation x4, local copies, waits for them, and re-layouts, window(): return jnp.stack(pieces, axis=1)  12.7 us
    unnamed x37, local copies, waits for them, and re-layouts  10.9 us
    ppermute x2, starting transfers between devices, extended(): after = lax.ppermute(initial, axis, down)  6.98 us
    ppermute x2, starting transfers between devices, extended(): before = lax.ppermute(last, axis, up)  6.51 us
    ppermute x4, waiting for transfers between devices, swapped(): lax.ppermute(shard, axis, [(i, i ^ 1 << apart) for i in range(lax.axis_si...  5.77 us
    gather x2, local copies, waits for them, and re-layouts, cousins(): return jnp.take(flat, slots, axis=0)  5.17 us
  transfers between devices with their start and end apart: 32, of which 13 were waited for; matrix products, arithmetic and copies ran while one was open for 16% of the time, Pallas kernels for 0%

commit v1 on v0

v1 whole, which is shorter than its diff:
```python
import jax
import jax.numpy as jnp
from jax import lax
from jax.experimental import pallas as pl
from jax.experimental.pallas import tpu as pltpu
from jax.sharding import PartitionSpec as P

F32, BF16 = jnp.float32, jnp.bfloat16
SLOTS, ROWS, LEAF, NRHS, RANK = 27, 16, 512, 256, 128
PART = NRHS // 4
TILE = 256


def cousin_positions():
    table = {}
    for i in range(2):
        for j in range(2):
            table[i, j] = [
                (big_a, big_b)
                for big_a in range(6)
                for big_b in range(6)
                if not (abs(big_a - 2 - i) <= 1 and abs(big_b - 2 - j) <= 1)
            ]
    return table


POSITIONS = cousin_positions()


def pick(value, i, j):
    v00, v01, v10, v11 = (value[0, 0], value[0, 1], value[1, 0], value[1, 1])
    return v00 + i * (v10 - v00) + j * (v01 - v00) + i * j * (v11 - v10 - v01 + v00)


def place(slot, i, j):
    big_a = pick({k: t[slot][0] for k, t in POSITIONS.items()}, i, j)
    big_b = pick({k: t[slot][1] for k, t in POSITIONS.items()}, i, j)
    return big_a, big_b


def dot(a, b, contract):
    return lax.dot_general(a, b, ((contract[:1], contract[1:]), ((), ())), preferred_element_type=F32)


def kernel(
    x_hbm, near_hbm, basis_hbm, transfer_hbm, leaf_hbm, top_hbm, out_hbm,
    near, basis, transfer, cl, ct, n, w, term, rb, t, lt, acc, out,
    local_sem, send_sem, recv_sem,
):
    a, b = lax.axis_index("gx"), lax.axis_index("gy")
    y, x = a // 4, a % 4
    z, c = b // 2, b % 2
    xh, alpha = x // 2, x % 2
    zz, zp = z // 2, z % 2
    mine = 2 * alpha + c

    def device(y, x, z, c):
        return (y * 4 + x, z * 2 + c)

    def flip(v, by):
        high, low = v // 2, v % 2
        return 2 * ((high + by // 2) % 2) + (low + by % 2) % 2

    locals_ = []

    def local(src, dst):
        copy = pltpu.make_async_copy(src, dst, local_sem.at[len(locals_)])
        copy.start()
        locals_.append(copy)
        return copy

    load_x = local(x_hbm.at[0, 0], n.at[4])
    load_basis = local(basis_hbm.at[0, 0], basis)
    load_transfer = local(transfer_hbm.at[0, 0], transfer)
    my_rows = pl.ds(pl.multiple_of(mine * 32, 32), 32)
    load_ct = local(top_hbm.at[0, 0], ct.at[:, my_rows, :])
    load_cl = local(leaf_hbm.at[0, 0], cl)
    load_near = local(near_hbm.at[0, 0], near)

    ring = [(dx, dc) for dx in range(4) for dc in range(2) if (dx, dc) != (0, 0)]
    ring_device = {k: device(y, flip(x, k[0]), z, (c + k[1]) % 2) for k in ring}
    up_y, down_y = device((y + 1) % 4, x, z, c), device((y + 3) % 4, x, z, c)
    window = [(e, g) for e in (-1, 0, 1) for g in range(2) if (e, g) != (0, 0)]
    window_device = {
        (e, g): device(y, x, 2 * ((zz + 4 + e) % 4) + (zp + g) % 2, c) for e, g in window
    }
    next_a, prev_a = ((a + 1) % 16, b), ((a + 15) % 16, b)
    next_b, prev_b = (a, (b + 1) % 16), (a, (b + 15) % 16)
    next_z, prev_z = device(y, x, (z + 1) % 8, c), device(y, x, (z + 7) % 8, c)
    greeted = (
        [ring_device[k] for k in ring]
        + [up_y, down_y]
        + [window_device[k] for k in window]
        + [next_a, prev_a, next_b, prev_b, next_z, prev_z]
    )
    barrier = pltpu.get_barrier_semaphore()
    for partner in greeted:
        pl.semaphore_signal(barrier, inc=1, device_id=partner, device_id_type=pl.DeviceIdType.MESH)

    sent = []

    def send(src, dst, to):
        k = len(sent)
        copy = pltpu.make_async_remote_copy(
            src_ref=src, dst_ref=dst, send_sem=send_sem.at[k], recv_sem=recv_sem.at[k],
            device_id=to, device_id_type=pl.DeviceIdType.MESH,
        )
        copy.start()
        sent.append(copy)
        return copy

    n[9] = jnp.zeros((LEAF, NRHS), BF16)
    w[12, 0] = jnp.zeros((RANK, NRHS), BF16)
    t[6, 0] = jnp.zeros((PART, RANK), BF16)

    load_x.wait()
    load_basis.wait()
    moments = dot(basis[...], n[4], (0, 0)).astype(BF16)
    own_row = c * 6 + 2 + alpha
    w[own_row, 1] = moments
    load_transfer.wait()
    terms = dot(moments, transfer[...], (0, 0)).astype(BF16)
    term[...] = terms.reshape(4, PART, RANK)
    rb[xh, mine] = term[mine]
    load_ct.wait()

    pl.semaphore_wait(barrier, len(greeted))

    top_term = [
        send(
            term.at[2 * ((alpha + dx % 2) % 2) + (c + dc) % 2],
            rb.at[xh, mine],
            ring_device[dx, dc],
        )
        for dx, dc in ring
    ]
    moments_z = [
        send(w.at[own_row, 1], w.at[own_row, 0], next_z),
        send(w.at[own_row, 1], w.at[own_row, 2], prev_z),
    ]
    charges_b = [send(n.at[4], n.at[3], next_b), send(n.at[4], n.at[5], prev_b)]
    charges_a = [send(n.at[4], n.at[1], next_a), send(n.at[4], n.at[7], prev_a)]
    quarter_c = send(ct.at[:, my_rows, :], ct.at[:, my_rows, :], ring_device[0, 1])
    quarter_x = send(ct.at[:, my_rows, :], ct.at[:, my_rows, :], ring_device[1, 0])

    def charge_at(u, v):
        va, vb = a + u - 1, b + v - 1
        inside = (va >= 0) & (va < 16) & (vb >= 0) & (vb < 16)
        return jnp.where(inside, 3 * u + v, 9)

    def near_add(blocks, first=False):
        @pl.loop(0, LEAF // TILE)
        def _(i):
            rows = pl.ds(pl.multiple_of(i * TILE, TILE), TILE)
            total = None if first else acc[rows, :]
            for u, v in blocks:
                product = dot(near[u, v, rows, :], n[charge_at(u, v)], (1, 0))
                total = product if total is None else total + product
            acc[rows, :] = total

    load_near.wait()
    near_add([(1, 1)], first=True)

    for copy in top_term:
        copy.wait_recv()
    for h in range(2):
        total = rb[h, 0].astype(F32)
        for j in range(1, 4):
            total = total + rb[h, j].astype(F32)
        t[2 + zp, 2 + h] = total.astype(BF16)
    top_z = [
        send(t.at[2 + zp, pl.ds(2, 2)], t.at[2 - 2 * e + zp, pl.ds(2, 2)], window_device[e, g])
        for e, g in window
    ]

    for copy in moments_z:
        copy.wait_recv()
    moments_x = []
    for dx in (1, 2, 3):
        far = (xh + dx // 2) % 2
        moments_x.append(
            send(w.at[own_row], w.at[c * 6 + x + 2 * (1 - far)], ring_device[dx, 0])
        )
    moments_c = [send(w.at[own_row], w.at[own_row], ring_device[0, 1])]

    for copy in top_z:
        copy.wait_recv()
    top_y = [
        send(t.at[pl.ds(0, 6), pl.ds(2, 2)], t.at[pl.ds(0, 6), pl.ds(0, 2)], up_y),
        send(t.at[pl.ds(0, 6), pl.ds(2, 2)], t.at[pl.ds(0, 6), pl.ds(4, 2)], down_y),
    ]

    corners = []
    for u, copy in zip((0, 2), charges_a):
        copy.wait_recv()
        corners.append(send(n.at[3 * u + 1], n.at[3 * u], next_b))
        corners.append(send(n.at[3 * u + 1], n.at[3 * u + 2], prev_b))
    near_add([(0, 1), (2, 1)])

    for dx, copy in zip((1, 2, 3), moments_x):
        copy.wait_recv()
    send_to = (((y + 1 + 2 * xh) % 4) * 4 + x, b)
    moments_y = send(
        w.at[pl.ds(c * 6 + 4 - 4 * xh, 2)], w.at[pl.ds(c * 6 + 4 * xh, 2)], send_to
    )
    for dx in (1, 2, 3):
        row = c * 6 + flip(x, dx) + 2 * (1 - xh)
        moments_c.append(send(w.at[row], w.at[row], ring_device[0, 1]))

    quarter_c.wait_recv()
    quarter_x.wait_recv()
    other_rows = pl.ds(pl.multiple_of((2 * (1 - alpha) + c) * 32, 32), 32)
    quarter_d = send(ct.at[:, other_rows, :], ct.at[:, other_rows, :], ring_device[0, 1])

    for copy in charges_b:
        copy.wait_recv()
    near_add([(1, 0), (1, 2)])

    quarter_d.wait_recv()
    for copy in top_y:
        copy.wait_recv()
    quarter = None
    for s in range(SLOTS):
        big_p, big_q = place(s, xh, zp)
        vp, vq = 2 * y - 2 + big_p, 2 * zz - 2 + big_q
        inside = (vp >= 0) & (vp < 8) & (vq >= 0) & (vq < 8)
        box = t[jnp.where(inside, big_q, 6), jnp.where(inside, big_p, 0)]
        product = dot(box, ct[s], (1, 1))
        quarter = product if quarter is None else quarter + product
    lt[mine] = quarter.astype(BF16)
    siblings = [(0, 1), (1, 0), (1, 1)]
    expansion = [send(lt.at[mine], lt.at[mine], ring_device[k]) for k in siblings]

    moments_y.wait_recv()
    rows_y = pl.ds(c * 6 + 4 * xh, 2)
    moments_c.append(send(w.at[rows_y], w.at[rows_y], ring_device[0, 1]))

    for copy in corners:
        copy.wait_recv()
    near_add([(0, 0), (0, 2), (2, 0), (2, 2)])

    load_cl.wait()
    for copy in moments_c:
        copy.wait_recv()
    local_leaf = None
    for s in range(SLOTS):
        big_a, big_b = place(s, alpha, c)
        va, vb = a - alpha - 2 + big_a, b - c - 2 + big_b
        inside = (va >= 0) & (va < 16) & (vb >= 0) & (vb < 16)
        row = jnp.where(inside, (big_b % 2) * 6 + big_a, 12)
        product = dot(cl[s], w[row, jnp.where(inside, big_b // 2, 0)], (1, 0))
        local_leaf = product if local_leaf is None else local_leaf + product

    for copy in expansion:
        copy.wait_recv()
    full = lt[...].reshape(NRHS, RANK)
    total = (local_leaf + dot(transfer[...], full, (1, 1))).astype(BF16)
    stores = []
    for i in range(LEAF // TILE):
        rows = pl.ds(i * TILE, TILE)
        out[rows, :] = (acc[rows, :] + dot(basis[rows, :], total, (1, 0))).astype(BF16)
        stores.append(local(out.at[rows, :], out_hbm.at[0, 0, rows, :]))

    for copy in sent:
        copy.wait_send()
    for copy in stores:
        copy.wait()


def shards(charges, near_blocks, basis, transfer, coupling_leaf, coupling_top):
    any_space = pl.BlockSpec(memory_space=pl.ANY)
    return pl.pallas_call(
        kernel,
        out_shape=jax.ShapeDtypeStruct((1, 1, LEAF, NRHS), BF16),
        in_specs=[any_space] * 6,
        out_specs=any_space,
        scratch_shapes=[
            pltpu.VMEM((3, 3, LEAF, LEAF), BF16),
            pltpu.VMEM((LEAF, RANK), BF16),
            pltpu.VMEM((RANK, RANK), BF16),
            pltpu.VMEM((SLOTS, RANK, RANK), BF16),
            pltpu.VMEM((SLOTS, RANK, RANK), BF16),
            pltpu.VMEM((10, LEAF, NRHS), BF16),
            pltpu.VMEM((13, 3, RANK, NRHS), BF16),
            pltpu.VMEM((4, PART, RANK), BF16),
            pltpu.VMEM((2, 4, PART, RANK), BF16),
            pltpu.VMEM((7, 6, PART, RANK), BF16),
            pltpu.VMEM((4, PART, RANK), BF16),
            pltpu.VMEM((LEAF, NRHS), F32),
            pltpu.VMEM((LEAF, NRHS), BF16),
            pltpu.SemaphoreType.DMA((8,)),
            pltpu.SemaphoreType.DMA((48,)),
            pltpu.SemaphoreType.DMA((48,)),
        ],
        compiler_params=pltpu.CompilerParams(
            collective_id=0, has_side_effects=True, vmem_limit_bytes=48 * 1024 * 1024
        ),
        cost_estimate=pl.CostEstimate(
            flops=1_600_000_000, bytes_accessed=6_500_000, transcendentals=0
        ),
    )(charges, near_blocks, basis, transfer, coupling_leaf, coupling_top)


def solution(mesh):
    return jax.shard_map(
        shards,
        mesh=mesh,
        in_specs=(
            P("gx", "gy", None, None),
            P("gx", "gy", None, None, None, None),
            P("gx", "gy", None, None),
            P("gx", "gy", None, None),
            P("gx", "gy", None, None, None),
            P("gx", "gy", None, None, None),
        ),
        out_specs=P("gx", "gy", None, None),
        check_vma=False,
    )
```

time: 222 us -> 52.7 us (0.24)
  the two profiles are of different devices: /device:TPU:80 before, /device:TPU:1 now
where the time goes in v1:
time: 52.7 us; the launch traced here: 52.4 us
  Pallas kernels  47 us (89%)
  local copies, waits for them, and re-layouts  5.42 us (10%)
    pallas_call x1, Pallas kernels, shards(): pl.pallas_call(kernel, out_shape=jax.ShapeDtypeStruct((1, 1, LEAF, NRHS),...  47 us
    unnamed x11, local copies, waits for them, and re-layouts  5.42 us

profile of v1, /device:TPU:1, one launch (start us, length us, event | category | flops | bytes accessed | tf_op | source)
XLA Modules:
  0.0 52.4 jit_solution(2865336218232004557)
XLA Ops:
  0.0 0.0 copy-start
  0.0 1.2 %copy-done = bf16[1,1,27,128,128]{4,3,2,1,0:T(8,128)(2,1)S(1)} copy-done((bf16[1,1,27,128,128]{4,3,2,1,0:T(8,128)(2,1)S(1)}, bf16[1,1,27,128,128]{4,3,2,1,0:T(8,128)(2,1)}, u32[]{:S(2)}) %copy-start) | copy-done | bytes 884760
  1.2 0.0 copy-start.1
  1.2 0.9 %copy-done.1 = bf16[1,1,512,256]{3,2,1,0:T(8,128)(2,1)S(1)} copy-done((bf16[1,1,512,256]{3,2,1,0:T(8,128)(2,1)S(1)}, bf16[1,1,512,256]{3,2,1,0:T(8,128)(2,1)}, u32[]{:S(2)}) %copy-start.1) | copy-done | bytes 262168
  2.1 0.0 copy-start.2
  2.1 0.9 %copy-done.2 = bf16[1,1,27,32,128]{4,3,2,1,0:T(8,128)(2,1)S(1)} copy-done((bf16[1,1,27,32,128]{4,3,2,1,0:T(8,128)(2,1)S(1)}, bf16[1,1,27,32,128]{4,3,2,1,0:T(8,128)(2,1)}, u32[]{:S(2)}) %copy-start.2) | copy-done | bytes 221208
  3.1 0.0 copy-start.3
  3.1 0.9 %copy-done.3 = bf16[1,1,512,128]{3,2,1,0:T(8,128)(2,1)S(1)} copy-done((bf16[1,1,512,128]{3,2,1,0:T(8,128)(2,1)S(1)}, bf16[1,1,512,128]{3,2,1,0:T(8,128)(2,1)}, u32[]{:S(2)}) %copy-start.3) | copy-done | bytes 131096
  4.0 0.0 copy-start.4
  4.0 0.8 %copy-done.4 = bf16[1,1,128,128]{3,2,1,0:T(8,128)(2,1)S(1)} copy-done((bf16[1,1,128,128]{3,2,1,0:T(8,128)(2,1)S(1)}, bf16[1,1,128,128]{3,2,1,0:T(8,128)(2,1)}, u32[]{:S(2)}) %copy-start.4) | copy-done | bytes 32792
  4.7 47.0 %shard_map.64 = bf16[1,1,512,256]{3,2,1,0:T(8,128)(2,1)S(1)} custom-call(bf16[1,1,512,256]{3,2,1,0:T(8,128)(2,1)S(1)} %copy-done.1, bf16[1,1,3,3,512,512]{5,4,3,2,1,0:T(8,128)(2,1)} %near_hbm.1, bf16[1,1,512,128]{3,2,1,0:T(8,128)(2,1)S(1)} %copy-done.3, bf16[1,1,128,128]{3,2,1,0:T(8,128)(2,1)S(1)} %copy-done.4, bf16[1,1,27,128,128]{4,3,2,1,0:T(8,128)(2,1)S(1)} %copy-done, ...), custom_call_target="tpu_custom_call" | custom-call | flops 1600000000 | bytes 6500000 | tf_op jit(solution)/shard_map/pallas_call | solution.py:272
  51.7 0.7 %copy.8 = bf16[1,1,512,256]{3,2,1,0:T(8,128)(2,1)} copy(bf16[1,1,512,256]{3,2,1,0:T(8,128)(2,1)S(1)} %shard_map.64) | data formatting | bytes 524288
Async XLA Ops:
  0.0 1.2 %copy-start = (bf16[1,1,27,128,128]{4,3,2,1,0:T(8,128)(2,1)S(1)}, bf16[1,1,27,128,128]{4,3,2,1,0:T(8,128)(2,1)}, u32[]{:S(2)}) copy-start(bf16[1,1,27,128,128]{4,3,2,1,0:T(8,128)(2,1)} %leaf_hbm.1) | copy-start | bytes 2654212
  1.2 0.9 %copy-start.1 = (bf16[1,1,512,256]{3,2,1,0:T(8,128)(2,1)S(1)}, bf16[1,1,512,256]{3,2,1,0:T(8,128)(2,1)}, u32[]{:S(2)}) copy-start(bf16[1,1,512,256]{3,2,1,0:T(8,128)(2,1)} %x_hbm.1) | copy-start | bytes 786436
  2.1 0.9 %copy-start.2 = (bf16[1,1,27,32,128]{4,3,2,1,0:T(8,128)(2,1)S(1)}, bf16[1,1,27,32,128]{4,3,2,1,0:T(8,128)(2,1)}, u32[]{:S(2)}) copy-start(bf16[1,1,27,32,128]{4,3,2,1,0:T(8,128)(2,1)} %top_hbm.1) | copy-start | bytes 663556
  3.1 0.9 %copy-start.3 = (bf16[1,1,512,128]{3,2,1,0:T(8,128)(2,1)S(1)}, bf16[1,1,512,128]{3,2,1,0:T(8,128)(2,1)}, u32[]{:S(2)}) copy-start(bf16[1,1,512,128]{3,2,1,0:T(8,128)(2,1)} %basis_hbm.1) | copy-start | bytes 393220
  4.0 0.8 %copy-start.4 = (bf16[1,1,128,128]{3,2,1,0:T(8,128)(2,1)S(1)}, bf16[1,1,128,128]{3,2,1,0:T(8,128)(2,1)}, u32[]{:S(2)}) copy-start(bf16[1,1,128,128]{3,2,1,0:T(8,128)(2,1)} %transfer_hbm.1) | copy-start | bytes 98308

commit v2 on v1

--- a/solution.py
+++ b/solution.py
@@ -42,6 +42,30 @@
     return lax.dot_general(a, b, ((contract[:1], contract[1:]), ((), ())), preferred_element_type=F32)
 
 
+class Copy:
+    def __init__(self, make, goes, comes):
+        self.make, self.goes, self.comes = make, goes, comes
+
+    def _if(self, condition, act):
+        if condition is True:
+            act()
+        else:
+            pl.when(condition)(act)
+
+    def start(self):
+        self._if(self.goes, lambda: self.make().start())
+
+    def wait_recv(self):
+        self._if(self.comes, lambda: self.make().wait_recv())
+
+    def wait_send(self):
+        self._if(self.goes, lambda: self.make().wait_send())
+
+
+def both(p, q):
+    return q if p is True else p if q is True else p & q
+
+
 def kernel(
     x_hbm, near_hbm, basis_hbm, transfer_hbm, leaf_hbm, top_hbm, out_hbm,
     near, basis, transfer, cl, ct, n, w, term, rb, t, lt, acc, out,
@@ -69,41 +93,70 @@
         locals_.append(copy)
         return copy
 
+    ring = [(dx, dc) for dx in (1, 3, 2, 0) for dc in range(2) if (dx, dc) != (0, 0)]
+    ring_device = {k: device(y, flip(x, k[0]), z, (c + k[1]) % 2) for k in ring}
+    core = ring_device[0, 1]
+    up, down = y < 3, y > 0
+    up_y, down_y = device((y + 1) % 4, x, z, c), device((y + 3) % 4, x, z, c)
+    over = ((xh == 1) & up) | ((xh == 0) & down)
+    over_device = [
+        device((y + 3 + 2 * xh) % 4, flip(x, 2 + g), z, c) for g in range(2)
+    ]
+    window = [(0, 1), (-1, 0), (-1, 1), (1, 0), (1, 1)]
+    window_device = {
+        (e, g): device(y, x, 2 * ((zz + 4 + e) % 4) + (zp + g) % 2, c) for e, g in window
+    }
+    window_goes = {-1: zz > 0, 0: True, 1: zz < 3}
+    window_comes = {-1: zz < 3, 0: True, 1: zz > 0}
+    next_a, prev_a = ((a + 1) % 16, b), ((a + 15) % 16, b)
+    next_b, prev_b = (a, (b + 1) % 16), (a, (b + 15) % 16)
+    next_z, prev_z = device(y, x, (z + 1) % 8, c), device(y, x, (z + 7) % 8, c)
+    far_b = device(y, x, (z + 7 + 2 * c) % 8, 1 - c)
+    far = ((c == 1) & (z < 7)) | ((c == 0) & (z > 0))
+
+    barrier = pltpu.get_barrier_semaphore()
+
+    def greet(partners):
+        for partner in partners:
+            pl.semaphore_signal(
+                barrier, inc=1, device_id=partner, device_id_type=pl.DeviceIdType.MESH
+            )
+
+    pl.when(zz > 0)(lambda: greet([window_device[-1, 0], window_device[-1, 1]]))
+    pl.when(zz < 3)(lambda: greet([window_device[1, 0], window_device[1, 1]]))
+    greet([window_device[0, 1]])
+    pl.when(up)(lambda: greet([up_y]))
+    pl.when(down)(lambda: greet([down_y]))
+    pl.when(over)(lambda: greet(over_device))
+    pl.when(far)(lambda: greet([far_b]))
+    greet([ring_device[k] for k in ring])
+
+    def one(condition):
+        return jnp.where(condition, 1, 0)
+
+    expected = (
+        8 + 2 * one(zz > 0) + 2 * one(zz < 3) + one(up) + one(down) + 2 * one(over) + one(far)
+    )
+
     load_x = local(x_hbm.at[0, 0], n.at[4])
     load_basis = local(basis_hbm.at[0, 0], basis)
     load_transfer = local(transfer_hbm.at[0, 0], transfer)
     my_rows = pl.ds(pl.multiple_of(mine * 32, 32), 32)
     load_ct = local(top_hbm.at[0, 0], ct.at[:, my_rows, :])
+    load_near = local(near_hbm.at[0, 0], near)
     load_cl = local(leaf_hbm.at[0, 0], cl)
-    load_near = local(near_hbm.at[0, 0], near)
-
-    ring = [(dx, dc) for dx in range(4) for dc in range(2) if (dx, dc) != (0, 0)]
-    ring_device = {k: device(y, flip(x, k[0]), z, (c + k[1]) % 2) for k in ring}
-    up_y, down_y = device((y + 1) % 4, x, z, c), device((y + 3) % 4, x, z, c)
-    window = [(e, g) for e in (-1, 0, 1) for g in range(2) if (e, g) != (0, 0)]
-    window_device = {
-        (e, g): device(y, x, 2 * ((zz + 4 + e) % 4) + (zp + g) % 2, c) for e, g in window
-    }
-    next_a, prev_a = ((a + 1) % 16, b), ((a + 15) % 16, b)
-    next_b, prev_b = (a, (b + 1) % 16), (a, (b + 15) % 16)
-    next_z, prev_z = device(y, x, (z + 1) % 8, c), device(y, x, (z + 7) % 8, c)
-    greeted = (
-        [ring_device[k] for k in ring]
-        + [up_y, down_y]
-        + [window_device[k] for k in window]
-        + [next_a, prev_a, next_b, prev_b, next_z, prev_z]
-    )
-    barrier = pltpu.get_barrier_semaphore()
-    for partner in greeted:
-        pl.semaphore_signal(barrier, inc=1, device_id=partner, device_id_type=pl.DeviceIdType.MESH)
 
     sent = []
 
-    def send(src, dst, to):
+    def send(kind, src, dst, to, goes=True, comes=True):
         k = len(sent)
-        copy = pltpu.make_async_remote_copy(
-            src_ref=src, dst_ref=dst, send_sem=send_sem.at[k], recv_sem=recv_sem.at[k],
-            device_id=to, device_id_type=pl.DeviceIdType.MESH,
+        copy = Copy(
+            lambda: pltpu.make_async_remote_copy(
+                src_ref=src, dst_ref=dst, send_sem=send_sem.at[k], recv_sem=recv_sem.at[k],
+                device_id=to, device_id_type=pl.DeviceIdType.MESH,
+            ),
+            goes,
+            comes,
         )
         copy.start()
         sent.append(copy)
@@ -116,32 +169,70 @@
     load_x.wait()
     load_basis.wait()
     moments = dot(basis[...], n[4], (0, 0)).astype(BF16)
-    own_row = c * 6 + 2 + alpha
-    w[own_row, 1] = moments
+    own = 2 + alpha
+    w[c * 6 + own, 1] = moments
     load_transfer.wait()
     terms = dot(moments, transfer[...], (0, 0)).astype(BF16)
     term[...] = terms.reshape(4, PART, RANK)
     rb[xh, mine] = term[mine]
     load_ct.wait()
 
-    pl.semaphore_wait(barrier, len(greeted))
+    pl.semaphore_wait(barrier, expected)
 
     top_term = [
         send(
+            "top",
             term.at[2 * ((alpha + dx % 2) % 2) + (c + dc) % 2],
             rb.at[xh, mine],
             ring_device[dx, dc],
         )
         for dx, dc in ring
     ]
-    moments_z = [
-        send(w.at[own_row, 1], w.at[own_row, 0], next_z),
-        send(w.at[own_row, 1], w.at[own_row, 2], prev_z),
+    center = w.at[c * 6 + own, 1]
+    came_from = []
+    for dx in (1, 3, 2):
+        far_h = (xh + dx // 2) % 2
+        copy = send("mom", center, w.at[c * 6 + x + 2 * (1 - far_h), 1], ring_device[dx, 0])
+        came_from.append((flip(x, dx) + 2 * (1 - xh), copy, True))
+    for g in range(2):
+        copy = send(
+            "mom", center, w.at[c * 6 + alpha + 4 * (1 - xh), 1], over_device[g], over, over
+        )
+        came_from.append(((alpha + g) % 2 + 4 * xh, copy, over))
+
+    to_core = []
+
+    def along_z(row, there):
+        place_ = c * 6 + row
+        return (
+            row,
+            there,
+            send("mom", w.at[place_, 1], w.at[place_, 0], next_z, both(there, z < 7), both(there, z > 0)),
+            send("mom", w.at[place_, 1], w.at[place_, 2], prev_z, both(there, z > 0), both(there, z < 7)),
+        )
+
+    def across(row, there, from_prev, from_next):
+        from_prev.wait_recv()
+        from_next.wait_recv()
+        place_ = c * 6 + row
+        to_core.append(send("mom", w.at[place_], w.at[place_], core, there, there))
+
+    came_z = [along_z(own, True)]
+    charges_b = [
+        send("cha", n.at[4], n.at[3], next_b, b < 15, b > 0),
+        send("cha", n.at[4], n.at[5], prev_b, b > 0, b < 15),
     ]
-    charges_b = [send(n.at[4], n.at[3], next_b), send(n.at[4], n.at[5], prev_b)]
-    charges_a = [send(n.at[4], n.at[1], next_a), send(n.at[4], n.at[7], prev_a)]
-    quarter_c = send(ct.at[:, my_rows, :], ct.at[:, my_rows, :], ring_device[0, 1])
-    quarter_x = send(ct.at[:, my_rows, :], ct.at[:, my_rows, :], ring_device[1, 0])
+    halves = [pl.ds(h * LEAF // 2, LEAF // 2) for h in range(2)]
+    charges_a = [
+        (
+            half,
+            send("cha", n.at[4, half], n.at[1, half], next_a, a < 15, a > 0),
+            send("cha", n.at[4, half], n.at[7, half], prev_a, a > 0, a < 15),
+        )
+        for half in halves
+    ]
+    quarter_c = send("ctg", ct.at[:, my_rows, :], ct.at[:, my_rows, :], core)
+    quarter_x = send("ctg", ct.at[:, my_rows, :], ct.at[:, my_rows, :], ring_device[1, 0])
 
     def charge_at(u, v):
         va, vb = a + u - 1, b + v - 1
@@ -158,9 +249,6 @@
                 total = product if total is None else total + product
             acc[rows, :] = total
 
-    load_near.wait()
-    near_add([(1, 1)], first=True)
-
     for copy in top_term:
         copy.wait_recv()
     for h in range(2):
@@ -168,50 +256,78 @@
         for j in range(1, 4):
             total = total + rb[h, j].astype(F32)
         t[2 + zp, 2 + h] = total.astype(BF16)
-    top_z = [
-        send(t.at[2 + zp, pl.ds(2, 2)], t.at[2 - 2 * e + zp, pl.ds(2, 2)], window_device[e, g])
+    top_z = {
+        (e, g): send(
+            "top",
+            t.at[2 + zp, pl.ds(2, 2)],
+            t.at[2 - 2 * e + zp, pl.ds(2, 2)],
+            window_device[e, g],
+            window_goes[e],
+            window_comes[e],
+        )
         for e, g in window
-    ]
-
-    for copy in moments_z:
-        copy.wait_recv()
-    moments_x = []
-    for dx in (1, 2, 3):
-        far = (xh + dx // 2) % 2
-        moments_x.append(
-            send(w.at[own_row], w.at[c * 6 + x + 2 * (1 - far)], ring_device[dx, 0])
-        )
-    moments_c = [send(w.at[own_row], w.at[own_row], ring_device[0, 1])]
-
-    for copy in top_z:
-        copy.wait_recv()
-    top_y = [
-        send(t.at[pl.ds(0, 6), pl.ds(2, 2)], t.at[pl.ds(0, 6), pl.ds(0, 2)], up_y),
-        send(t.at[pl.ds(0, 6), pl.ds(2, 2)], t.at[pl.ds(0, 6), pl.ds(4, 2)], down_y),
-    ]
+    }
+
+    for row, copy, there in came_from[:3]:
+        copy.wait_recv()
+        came_z.append(along_z(row, there))
+
+    load_near.wait()
+    near_add([(1, 1)], first=True)
+
+    top_y = []
+
+    def along_y(pair, there):
+        columns = pl.ds(2 * pair, 2)
+        for rows, to, goes, comes in ((0, up_y, up, down), (4, down_y, down, up)):
+            top_y.append(
+                send(
+                    "top",
+                    t.at[columns, pl.ds(2, 2)],
+                    t.at[columns, pl.ds(rows, 2)],
+                    to,
+                    both(there, goes),
+                    both(there, comes),
+                )
+            )
+
+    top_z[0, 1].wait_recv()
+    along_y(1, True)
+    for row, copy, there in came_from[3:]:
+        copy.wait_recv()
+        came_z.append(along_z(row, there))
+    for e in (-1, 1):
+        top_z[e, 0].wait_recv()
+        top_z[e, 1].wait_recv()
+        along_y(1 - e, window_comes[e])
 
     corners = []
-    for u, copy in zip((0, 2), charges_a):
-        copy.wait_recv()
-        corners.append(send(n.at[3 * u + 1], n.at[3 * u], next_b))
-        corners.append(send(n.at[3 * u + 1], n.at[3 * u + 2], prev_b))
+
+    def corner(half, from_prev, from_next):
+        for u, copy, there in ((0, from_prev, a > 0), (2, from_next, a < 15)):
+            copy.wait_recv()
+            row = n.at[3 * u + 1, half]
+            corners.append(
+                send("cha", row, n.at[3 * u, half], next_b, there & (b < 15), there & (b > 0))
+            )
+            corners.append(
+                send("cha", row, n.at[3 * u + 2, half], prev_b, there & (b > 0), there & (b < 15))
+            )
+
+    corner(*charges_a[0])
+    across(*came_z[0])
+    across(*came_z[1])
+    corner(*charges_a[1])
     near_add([(0, 1), (2, 1)])
-
-    for dx, copy in zip((1, 2, 3), moments_x):
-        copy.wait_recv()
-    send_to = (((y + 1 + 2 * xh) % 4) * 4 + x, b)
-    moments_y = send(
-        w.at[pl.ds(c * 6 + 4 - 4 * xh, 2)], w.at[pl.ds(c * 6 + 4 * xh, 2)], send_to
-    )
-    for dx in (1, 2, 3):
-        row = c * 6 + flip(x, dx) + 2 * (1 - xh)
-        moments_c.append(send(w.at[row], w.at[row], ring_device[0, 1]))
+    across(*came_z[2])
+    across(*came_z[3])
 
     quarter_c.wait_recv()
     quarter_x.wait_recv()
     other_rows = pl.ds(pl.multiple_of((2 * (1 - alpha) + c) * 32, 32), 32)
-    quarter_d = send(ct.at[:, other_rows, :], ct.at[:, other_rows, :], ring_device[0, 1])
-
+    quarter_d = send("ctg", ct.at[:, other_rows, :], ct.at[:, other_rows, :], core)
+    across(*came_z[4])
+    across(*came_z[5])
     for copy in charges_b:
         copy.wait_recv()
     near_add([(1, 0), (1, 2)])
@@ -228,19 +344,11 @@
         product = dot(box, ct[s], (1, 1))
         quarter = product if quarter is None else quarter + product
     lt[mine] = quarter.astype(BF16)
-    siblings = [(0, 1), (1, 0), (1, 1)]
-    expansion = [send(lt.at[mine], lt.at[mine], ring_device[k]) for k in siblings]
-
-    moments_y.wait_recv()
-    rows_y = pl.ds(c * 6 + 4 * xh, 2)
-    moments_c.append(send(w.at[rows_y], w.at[rows_y], ring_device[0, 1]))
-
-    for copy in corners:
-        copy.wait_recv()
-    near_add([(0, 0), (0, 2), (2, 0), (2, 2)])
+    siblings = [(1, 0), (1, 1), (0, 1)]
+    expansion = [send("top", lt.at[mine], lt.at[mine], ring_device[k]) for k in siblings]
 
     load_cl.wait()
-    for copy in moments_c:
+    for copy in to_core:
         copy.wait_recv()
     local_leaf = None
     for s in range(SLOTS):
@@ -250,6 +358,10 @@
         row = jnp.where(inside, (big_b % 2) * 6 + big_a, 12)
         product = dot(cl[s], w[row, jnp.where(inside, big_b // 2, 0)], (1, 0))
         local_leaf = product if local_leaf is None else local_leaf + product
+
+    for copy in corners:
+        copy.wait_recv()
+    near_add([(0, 0), (0, 2), (2, 0), (2, 2)])
 
     for copy in expansion:
         copy.wait_recv()
@@ -289,11 +401,11 @@
             pltpu.VMEM((LEAF, NRHS), F32),
             pltpu.VMEM((LEAF, NRHS), BF16),
             pltpu.SemaphoreType.DMA((8,)),
-            pltpu.SemaphoreType.DMA((48,)),
-            pltpu.SemaphoreType.DMA((48,)),
+            pltpu.SemaphoreType.DMA((72,)),
+            pltpu.SemaphoreType.DMA((72,)),
         ],
         compiler_params=pltpu.CompilerParams(
-            collective_id=0, has_side_effects=True, vmem_limit_bytes=48 * 1024 * 1024
+            collective_id=0, has_side_effects=True, vmem_limit_bytes=60 * 1024 * 1024
         ),
         cost_estimate=pl.CostEstimate(
             flops=1_600_000_000, bytes_accessed=6_500_000, transcendentals=0

time: 52.7 us -> 34.1 us (0.65)
  the two profiles are of different devices: /device:TPU:1 before, /device:TPU:57 now
where the time goes in v2:
time: 34.1 us; the launch traced here: 34 us
  Pallas kernels  32.3 us (95%)
  local copies, waits for them, and re-layouts  1.67 us (5%)
    pallas_call x1, Pallas kernels, shards(): pl.pallas_call(kernel, out_shape=jax.ShapeDtypeStruct((1, 1, LEAF, NRHS),...  32.3 us
    unnamed x1, local copies, waits for them, and re-layouts  1.67 us

profile of v2, /device:TPU:57, one launch (start us, length us, event | category | flops | bytes accessed | tf_op | source)
XLA Modules:
  0.0 34.0 jit_solution(3108545687165389185)
XLA Ops:
  0.0 32.3 %shard_map.64 = bf16[1,1,512,256]{3,2,1,0:T(8,128)(2,1)} custom-call(bf16[1,1,512,256]{3,2,1,0:T(8,128)(2,1)} %x_hbm.1, bf16[1,1,3,3,512,512]{5,4,3,2,1,0:T(8,128)(2,1)} %near_hbm.1, bf16[1,1,512,128]{3,2,1,0:T(8,128)(2,1)} %basis_hbm.1, bf16[1,1,128,128]{3,2,1,0:T(8,128)(2,1)} %transfer_hbm.1, bf16[1,1,27,128,128]{4,3,2,1,0:T(8,128)(2,1)} %leaf_hbm.1, ...), custom_call_target="tpu_custom_call" | custom-call | flops 1600000000 | bytes 6500000 | tf_op jit(solution)/shard_map/pallas_call | solution.py:384
  32.3 1.7 %copy.8 = bf16[1,1,512,256]{3,2,1,0:T(8,128)(2,1)} copy(bf16[1,1,512,256]{3,2,1,0:T(8,128)(2,1)} %shard_map.64) | data formatting | bytes 524288

commit v3 on v2

--- a/solution.py
+++ b/solution.py
@@ -9,6 +9,7 @@
 SLOTS, ROWS, LEAF, NRHS, RANK = 27, 16, 512, 256, 128
 PART = NRHS // 4
 TILE = 256
+TURN = 64
 
 
 def cousin_positions():
@@ -67,8 +68,8 @@
 
 
 def kernel(
-    x_hbm, near_hbm, basis_hbm, transfer_hbm, leaf_hbm, top_hbm, out_hbm,
-    near, basis, transfer, cl, ct, n, w, term, rb, t, lt, acc, out,
+    x_hbm, near_hbm, basis_hbm, transfer_hbm, leaf_hbm, top_hbm, out,
+    near, basis, transfer, cl, ct, n, w, term, rb, t, lt, acc,
     local_sem, send_sem, recv_sem,
 ):
     a, b = lax.axis_index("gx"), lax.axis_index("gy")
@@ -93,7 +94,11 @@
         locals_.append(copy)
         return copy
 
-    ring = [(dx, dc) for dx in (1, 3, 2, 0) for dc in range(2) if (dx, dc) != (0, 0)]
+    load_x = local(x_hbm.at[0, 0], n.at[4])
+    load_basis = local(basis_hbm.at[0, 0], basis)
+    load_transfer = local(transfer_hbm.at[0, 0], transfer)
+
+    ring = [(dx, dc) for dx in (2, 1, 3, 0) for dc in range(2) if (dx, dc) != (0, 0)]
     ring_device = {k: device(y, flip(x, k[0]), z, (c + k[1]) % 2) for k in ring}
     core = ring_device[0, 1]
     up, down = y < 3, y > 0
@@ -138,17 +143,9 @@
         8 + 2 * one(zz > 0) + 2 * one(zz < 3) + one(up) + one(down) + 2 * one(over) + one(far)
     )
 
-    load_x = local(x_hbm.at[0, 0], n.at[4])
-    load_basis = local(basis_hbm.at[0, 0], basis)
-    load_transfer = local(transfer_hbm.at[0, 0], transfer)
-    my_rows = pl.ds(pl.multiple_of(mine * 32, 32), 32)
-    load_ct = local(top_hbm.at[0, 0], ct.at[:, my_rows, :])
-    load_near = local(near_hbm.at[0, 0], near)
-    load_cl = local(leaf_hbm.at[0, 0], cl)
-
     sent = []
 
-    def send(kind, src, dst, to, goes=True, comes=True):
+    def send(kind, src, dst, to, goes=True, comes=True, now=True):
         k = len(sent)
         copy = Copy(
             lambda: pltpu.make_async_remote_copy(
@@ -158,7 +155,8 @@
             goes,
             comes,
         )
-        copy.start()
+        if now:
+            copy.start()
         sent.append(copy)
         return copy
 
@@ -172,10 +170,13 @@
     own = 2 + alpha
     w[c * 6 + own, 1] = moments
     load_transfer.wait()
+    my_rows = pl.ds(pl.multiple_of(mine * 32, 32), 32)
+    load_ct = local(top_hbm.at[0, 0], ct.at[:, my_rows, :])
+    load_near = local(near_hbm.at[0, 0], near)
+    load_cl = local(leaf_hbm.at[0, 0], cl)
     terms = dot(moments, transfer[...], (0, 0)).astype(BF16)
     term[...] = terms.reshape(4, PART, RANK)
     rb[xh, mine] = term[mine]
-    load_ct.wait()
 
     pl.semaphore_wait(barrier, expected)
 
@@ -218,21 +219,34 @@
         to_core.append(send("mom", w.at[place_], w.at[place_], core, there, there))
 
     came_z = [along_z(own, True)]
-    charges_b = [
-        send("cha", n.at[4], n.at[3], next_b, b < 15, b > 0),
-        send("cha", n.at[4], n.at[5], prev_b, b > 0, b < 15),
-    ]
-    halves = [pl.ds(h * LEAF // 2, LEAF // 2) for h in range(2)]
-    charges_a = [
-        (
-            half,
-            send("cha", n.at[4, half], n.at[1, half], next_a, a < 15, a > 0),
-            send("cha", n.at[4, half], n.at[7, half], prev_a, a > 0, a < 15),
-        )
-        for half in halves
-    ]
+
+    first, *others = (
+        pl.ds(0, TURN),
+        pl.ds(TURN, (LEAF - TURN) // 2),
+        pl.ds((LEAF + TURN) // 2, (LEAF - TURN) // 2),
+    )
+    rest = pl.ds(TURN, LEAF - TURN)
+    side = 2 * c
+    turned = send("cha", n.at[4, first], n.at[5 - side, first], far_b, far, far)
+    unturned = send("cha", n.at[4, rest], n.at[5 - side, rest], far_b, far, far)
+    charges_a = []
+
+    def along_a(part):
+        charges_a.append(
+            (
+                part,
+                send("cha", n.at[4, part], n.at[1, part], next_a, a < 15, a > 0),
+                send("cha", n.at[4, part], n.at[7, part], prev_a, a > 0, a < 15),
+            )
+        )
+
+    for part in others:
+        along_a(part)
+    load_ct.wait()
+    quarter_x = send("ctg", ct.at[:, my_rows, :], ct.at[:, my_rows, :], ring_device[1, 0])
     quarter_c = send("ctg", ct.at[:, my_rows, :], ct.at[:, my_rows, :], core)
-    quarter_x = send("ctg", ct.at[:, my_rows, :], ct.at[:, my_rows, :], ring_device[1, 0])
+    along_a(first)
+    paired = send("cha", n.at[4], n.at[3 + side], core)
 
     def charge_at(u, v):
         va, vb = a + u - 1, b + v - 1
@@ -268,9 +282,15 @@
         for e, g in window
     }
 
-    for row, copy, there in came_from[:3]:
+    for row, copy, there in came_from:
         copy.wait_recv()
         came_z.append(along_z(row, there))
+
+    far_corners, core_corners = [], []
+    turned.wait_recv()
+    row = n.at[3 + side, first]
+    far_corners.append(send("cha", row, n.at[side, first], next_a, far & (a < 15), far & (a > 0)))
+    far_corners.append(send("cha", row, n.at[6 + side, first], prev_a, far & (a > 0), far & (a < 15)))
 
     load_near.wait()
     near_add([(1, 1)], first=True)
@@ -293,32 +313,25 @@
 
     top_z[0, 1].wait_recv()
     along_y(1, True)
-    for row, copy, there in came_from[3:]:
-        copy.wait_recv()
-        came_z.append(along_z(row, there))
     for e in (-1, 1):
         top_z[e, 0].wait_recv()
         top_z[e, 1].wait_recv()
         along_y(1 - e, window_comes[e])
 
-    corners = []
-
-    def corner(half, from_prev, from_next):
+    def corner(part, from_prev, from_next, over_z):
         for u, copy, there in ((0, from_prev, a > 0), (2, from_next, a < 15)):
             copy.wait_recv()
-            row = n.at[3 * u + 1, half]
-            corners.append(
-                send("cha", row, n.at[3 * u, half], next_b, there & (b < 15), there & (b > 0))
-            )
-            corners.append(
-                send("cha", row, n.at[3 * u + 2, half], prev_b, there & (b > 0), there & (b < 15))
-            )
-
-    corner(*charges_a[0])
+            row = n.at[3 * u + 1, part]
+            if over_z:
+                far_corners.append(
+                    send("cha", row, n.at[3 * u + 2 - side, part], far_b, there & far, there & far)
+                )
+            core_corners.append(send("cha", row, n.at[3 * u + side, part], core, there, there))
+
+    corner(*charges_a[0], True)
     across(*came_z[0])
     across(*came_z[1])
-    corner(*charges_a[1])
-    near_add([(0, 1), (2, 1)])
+    corner(*charges_a[1], True)
     across(*came_z[2])
     across(*came_z[3])
 
@@ -328,9 +341,11 @@
     quarter_d = send("ctg", ct.at[:, other_rows, :], ct.at[:, other_rows, :], core)
     across(*came_z[4])
     across(*came_z[5])
-    for copy in charges_b:
-        copy.wait_recv()
+    paired.wait_recv()
+    unturned.wait_recv()
     near_add([(1, 0), (1, 2)])
+    corner(*charges_a[2], False)
+    near_add([(0, 1), (2, 1)])
 
     quarter_d.wait_recv()
     for copy in top_y:
@@ -347,6 +362,10 @@
     siblings = [(1, 0), (1, 1), (0, 1)]
     expansion = [send("top", lt.at[mine], lt.at[mine], ring_device[k]) for k in siblings]
 
+    for copy in core_corners:
+        copy.wait_recv()
+    near_add([(0, 2 - side), (2, 2 - side)])
+
     load_cl.wait()
     for copy in to_core:
         copy.wait_recv()
@@ -359,33 +378,29 @@
         product = dot(cl[s], w[row, jnp.where(inside, big_b // 2, 0)], (1, 0))
         local_leaf = product if local_leaf is None else local_leaf + product
 
-    for copy in corners:
-        copy.wait_recv()
-    near_add([(0, 0), (0, 2), (2, 0), (2, 2)])
+    for copy in far_corners:
+        copy.wait_recv()
+    near_add([(0, side), (2, side)])
 
     for copy in expansion:
         copy.wait_recv()
     full = lt[...].reshape(NRHS, RANK)
     total = (local_leaf + dot(transfer[...], full, (1, 1))).astype(BF16)
-    stores = []
     for i in range(LEAF // TILE):
         rows = pl.ds(i * TILE, TILE)
-        out[rows, :] = (acc[rows, :] + dot(basis[rows, :], total, (1, 0))).astype(BF16)
-        stores.append(local(out.at[rows, :], out_hbm.at[0, 0, rows, :]))
+        out[0, 0, rows, :] = (acc[rows, :] + dot(basis[rows, :], total, (1, 0))).astype(BF16)
 
     for copy in sent:
         copy.wait_send()
-    for copy in stores:
-        copy.wait()
 
 
 def shards(charges, near_blocks, basis, transfer, coupling_leaf, coupling_top):
     any_space = pl.BlockSpec(memory_space=pl.ANY)
     return pl.pallas_call(
         kernel,
-        out_shape=jax.ShapeDtypeStruct((1, 1, LEAF, NRHS), BF16),
+        out_shape=pltpu.VMEM((1, 1, LEAF, NRHS), BF16),
         in_specs=[any_space] * 6,
-        out_specs=any_space,
+        out_specs=pl.BlockSpec(memory_space=pltpu.VMEM),
         scratch_shapes=[
             pltpu.VMEM((3, 3, LEAF, LEAF), BF16),
             pltpu.VMEM((LEAF, RANK), BF16),
@@ -399,7 +414,6 @@
             pltpu.VMEM((7, 6, PART, RANK), BF16),
             pltpu.VMEM((4, PART, RANK), BF16),
             pltpu.VMEM((LEAF, NRHS), F32),
-            pltpu.VMEM((LEAF, NRHS), BF16),
             pltpu.SemaphoreType.DMA((8,)),
             pltpu.SemaphoreType.DMA((72,)),
             pltpu.SemaphoreType.DMA((72,)),

time: 34.1 us -> 31.8 us (0.933)
  the two profiles are of different devices: /device:TPU:57 before, /device:TPU:91 now
where the time goes in v3:
time: 31.8 us; the launch traced here: 31.7 us
  Pallas kernels  31 us (97%)
  local copies, waits for them, and re-layouts  0.71 us (2%)
    pallas_call x1, Pallas kernels, shards(): pl.pallas_call(kernel, out_shape=pltpu.VMEM((1, 1, LEAF, NRHS), BF16), in...  31 us
    unnamed x1, local copies, waits for them, and re-layouts  0.71 us

profile of v3, /device:TPU:91, one launch (start us, length us, event | category | flops | bytes accessed | tf_op | source)
XLA Modules:
  0.0 31.7 jit_solution(6303242733012633214)
XLA Ops:
  0.0 31.0 %shard_map.64 = bf16[1,1,512,256]{3,2,1,0:T(8,128)(2,1)S(1)} custom-call(bf16[1,1,512,256]{3,2,1,0:T(8,128)(2,1)} %x_hbm.1, bf16[1,1,3,3,512,512]{5,4,3,2,1,0:T(8,128)(2,1)} %near_hbm.1, bf16[1,1,512,128]{3,2,1,0:T(8,128)(2,1)} %basis_hbm.1, bf16[1,1,128,128]{3,2,1,0:T(8,128)(2,1)} %transfer_hbm.1, bf16[1,1,27,128,128]{4,3,2,1,0:T(8,128)(2,1)} %leaf_hbm.1, ...), custom_call_target="tpu_custom_call" | custom-call | flops 1600000000 | bytes 6500000 | tf_op jit(solution)/shard_map/pallas_call | solution.py:399
  31.0 0.7 %copy.8 = bf16[1,1,512,256]{3,2,1,0:T(8,128)(2,1)} copy(bf16[1,1,512,256]{3,2,1,0:T(8,128)(2,1)S(1)} %shard_map.64) | data formatting | bytes 524288

commit v4 on v3

--- a/solution.py
+++ b/solution.py
@@ -70,7 +70,7 @@
 def kernel(
     x_hbm, near_hbm, basis_hbm, transfer_hbm, leaf_hbm, top_hbm, out,
     near, basis, transfer, cl, ct, n, w, term, rb, t, lt, acc,
-    local_sem, send_sem, recv_sem,
+    local_sem, send_sem, recv_sem, known_sem,
 ):
     a, b = lax.axis_index("gx"), lax.axis_index("gy")
     y, x = a // 4, a % 4
@@ -127,9 +127,8 @@
                 barrier, inc=1, device_id=partner, device_id_type=pl.DeviceIdType.MESH
             )
 
-    pl.when(zz > 0)(lambda: greet([window_device[-1, 0], window_device[-1, 1]]))
-    pl.when(zz < 3)(lambda: greet([window_device[1, 0], window_device[1, 1]]))
-    greet([window_device[0, 1]])
+    pl.when(z > 0)(lambda: greet([prev_z]))
+    pl.when(z < 7)(lambda: greet([next_z]))
     pl.when(up)(lambda: greet([up_y]))
     pl.when(down)(lambda: greet([down_y]))
     pl.when(over)(lambda: greet(over_device))
@@ -140,7 +139,7 @@
         return jnp.where(condition, 1, 0)
 
     expected = (
-        8 + 2 * one(zz > 0) + 2 * one(zz < 3) + one(up) + one(down) + 2 * one(over) + one(far)
+        7 + one(z > 0) + one(z < 7) + one(up) + one(down) + 2 * one(over) + one(far)
     )
 
     sent = []
@@ -213,8 +212,9 @@
         )
 
     def across(row, there, from_prev, from_next):
-        from_prev.wait_recv()
-        from_next.wait_recv()
+        if row is not own:
+            from_prev.wait_recv()
+            from_next.wait_recv()
         place_ = c * 6 + row
         to_core.append(send("mom", w.at[place_], w.at[place_], core, there, there))
 
@@ -270,6 +270,17 @@
         for j in range(1, 4):
             total = total + rb[h, j].astype(F32)
         t[2 + zp, 2 + h] = total.astype(BF16)
+    for copy in came_z[0][2:]:
+        copy.wait_recv()
+    pair = window_device[0, 1]
+    pl.when(((zp == 1) & (zz < 3)) | ((zp == 0) & (zz > 0)))(
+        lambda: pl.semaphore_signal(
+            known_sem, inc=1, device_id=pair, device_id_type=pl.DeviceIdType.MESH
+        )
+    )
+    pl.when(((zp == 0) & (zz < 3)) | ((zp == 1) & (zz > 0)))(
+        lambda: pl.semaphore_wait(known_sem, 1)
+    )
     top_z = {
         (e, g): send(
             "top",
@@ -378,17 +389,18 @@
         product = dot(cl[s], w[row, jnp.where(inside, big_b // 2, 0)], (1, 0))
         local_leaf = product if local_leaf is None else local_leaf + product
 
-    for copy in far_corners:
-        copy.wait_recv()
-    near_add([(0, side), (2, side)])
-
     for copy in expansion:
         copy.wait_recv()
     full = lt[...].reshape(NRHS, RANK)
     total = (local_leaf + dot(transfer[...], full, (1, 1))).astype(BF16)
+    for copy in far_corners:
+        copy.wait_recv()
     for i in range(LEAF // TILE):
         rows = pl.ds(i * TILE, TILE)
-        out[0, 0, rows, :] = (acc[rows, :] + dot(basis[rows, :], total, (1, 0))).astype(BF16)
+        result = acc[rows, :] + dot(basis[rows, :], total, (1, 0))
+        for u in (0, 2):
+            result = result + dot(near[u, side, rows, :], n[charge_at(u, side)], (1, 0))
+        out[0, 0, rows, :] = result.astype(BF16)
 
     for copy in sent:
         copy.wait_send()
@@ -415,8 +427,9 @@
             pltpu.VMEM((4, PART, RANK), BF16),
             pltpu.VMEM((LEAF, NRHS), F32),
             pltpu.SemaphoreType.DMA((8,)),
-            pltpu.SemaphoreType.DMA((72,)),
-            pltpu.SemaphoreType.DMA((72,)),
+            pltpu.SemaphoreType.DMA((96,)),
+            pltpu.SemaphoreType.DMA((96,)),
+            pltpu.SemaphoreType.REGULAR,
         ],
         compiler_params=pltpu.CompilerParams(
             collective_id=0, has_side_effects=True, vmem_limit_bytes=60 * 1024 * 1024

time: 31.8 us -> 31.6 us (level)
  the two profiles are of different devices: /device:TPU:91 before, /device:TPU:123 now
where the time goes in v4:
time: 31.6 us; the launch traced here: 31.5 us
  Pallas kernels  30.8 us (97%)
  local copies, waits for them, and re-layouts  0.71 us (2%)
    pallas_call x1, Pallas kernels, shards(): pl.pallas_call(kernel, out_shape=pltpu.VMEM((1, 1, LEAF, NRHS), BF16), in...  30.8 us
    unnamed x1, local copies, waits for them, and re-layouts  0.71 us

profile of v4, /device:TPU:123, one launch (start us, length us, event | category | flops | bytes accessed | tf_op | source)
XLA Modules:
  0.0 31.5 jit_solution(15692388181864582290)
XLA Ops:
  0.0 30.8 %shard_map.64 = bf16[1,1,512,256]{3,2,1,0:T(8,128)(2,1)S(1)} custom-call(bf16[1,1,512,256]{3,2,1,0:T(8,128)(2,1)} %x_hbm.1, bf16[1,1,3,3,512,512]{5,4,3,2,1,0:T(8,128)(2,1)} %near_hbm.1, bf16[1,1,512,128]{3,2,1,0:T(8,128)(2,1)} %basis_hbm.1, bf16[1,1,128,128]{3,2,1,0:T(8,128)(2,1)} %transfer_hbm.1, bf16[1,1,27,128,128]{4,3,2,1,0:T(8,128)(2,1)} %leaf_hbm.1, ...), custom_call_target="tpu_custom_call" | custom-call | flops 1600000000 | bytes 6500000 | tf_op jit(solution)/shard_map/pallas_call | solution.py:411
  30.8 0.7 %copy.8 = bf16[1,1,512,256]{3,2,1,0:T(8,128)(2,1)} copy(bf16[1,1,512,256]{3,2,1,0:T(8,128)(2,1)S(1)} %shard_map.64) | data formatting | bytes 524288

commit v5 on v4

--- a/solution.py
+++ b/solution.py
@@ -263,6 +263,15 @@
                 total = product if total is None else total + product
             acc[rows, :] = total
 
+    for copy in came_z[0][2:]:
+        copy.wait_recv()
+    pair = window_device[0, 1]
+    pl.when(((zp == 1) & (zz < 3)) | ((zp == 0) & (zz > 0)))(
+        lambda: pl.semaphore_signal(
+            known_sem, inc=1, device_id=pair, device_id_type=pl.DeviceIdType.MESH
+        )
+    )
+
     for copy in top_term:
         copy.wait_recv()
     for h in range(2):
@@ -270,14 +279,6 @@
         for j in range(1, 4):
             total = total + rb[h, j].astype(F32)
         t[2 + zp, 2 + h] = total.astype(BF16)
-    for copy in came_z[0][2:]:
-        copy.wait_recv()
-    pair = window_device[0, 1]
-    pl.when(((zp == 1) & (zz < 3)) | ((zp == 0) & (zz > 0)))(
-        lambda: pl.semaphore_signal(
-            known_sem, inc=1, device_id=pair, device_id_type=pl.DeviceIdType.MESH
-        )
-    )
     pl.when(((zp == 0) & (zz < 3)) | ((zp == 1) & (zz > 0)))(
         lambda: pl.semaphore_wait(known_sem, 1)
     )

time: 31.6 us -> 31.6 us (level)
  no operation moved by 1% of the time
where the time goes in v5:
time: 31.6 us; the launch traced here: 31.5 us
  Pallas kernels  30.8 us (97%)
  local copies, waits for them, and re-layouts  0.71 us (2%)
    pallas_call x1, Pallas kernels, shards(): pl.pallas_call(kernel, out_shape=pltpu.VMEM((1, 1, LEAF, NRHS), BF16), in...  30.8 us
    unnamed x1, local copies, waits for them, and re-layouts  0.71 us

profile of v5, /device:TPU:123, one launch (start us, length us, event | category | flops | bytes accessed | tf_op | source)
XLA Modules:
  0.0 31.5 jit_solution(7190300557600792944)
XLA Ops:
  0.0 30.8 %shard_map.64 = bf16[1,1,512,256]{3,2,1,0:T(8,128)(2,1)S(1)} custom-call(bf16[1,1,512,256]{3,2,1,0:T(8,128)(2,1)} %x_hbm.1, bf16[1,1,3,3,512,512]{5,4,3,2,1,0:T(8,128)(2,1)} %near_hbm.1, bf16[1,1,512,128]{3,2,1,0:T(8,128)(2,1)} %basis_hbm.1, bf16[1,1,128,128]{3,2,1,0:T(8,128)(2,1)} %transfer_hbm.1, bf16[1,1,27,128,128]{4,3,2,1,0:T(8,128)(2,1)} %leaf_hbm.1, ...), custom_call_target="tpu_custom_call" | custom-call | flops 1600000000 | bytes 6500000 | tf_op jit(solution)/shard_map/pallas_call | solution.py:412
  30.8 0.7 %copy.8 = bf16[1,1,512,256]{3,2,1,0:T(8,128)(2,1)} copy(bf16[1,1,512,256]{3,2,1,0:T(8,128)(2,1)S(1)} %shard_map.64) | data formatting | bytes 524288
